TPU v7x, 32 devices: a whole 2x2x4 slice. The times are simulated.
32 devices in a mesh: row: 4 (over z), col: 8 (over y, x, core).
Axes of the slice: x: 2, y: 2, z: 4, core: 2. Of those that a mesh axis runs over, the one named last changes fastest.
Arguments:
- mask_field: float32 [1536, 3072], P('row', 'col'), may hold values from -1 to 1
- resist_goal: float32 [1536, 3072], P('row', 'col'), may hold values from 0 to 1
- kernels: float32 [8, 2, 64, 64], replicated, may hold values from -30 to 30
- colour: int32 [4, 8], P('row', 'col'), may hold values from 0 to 3
- active: int32 [4, 8], P('row', 'col'), may hold values 0 or 1
Outputs:
- final_mask: float32 [1536, 3072], P('row', 'col')
- next_tiles: float32 [2048, 4096], P('row', 'col')
Inputs may be any that keep to these rules, and one draw needn't show every extreme that they name: Every entry of `colour` is 0, 1, 2 or 3, and neighbouring tiles may have the same colour.
All inputs are finite; a program needn't handle non-finite values. No bound on the sum of `active` on one device may be relied on, other than what follows from the above.
Results may differ from a plain program's by a relative error of at most 0.0035.
Values may be sent and summed in bfloat16 or wider, within the bound.
A program may use at most 64 MiB of HBM per device.

v0:
```python
import functools
import math

import jax
import jax.numpy as jnp
import numpy as np
from jax import lax
from jax.experimental import pallas as pl
from jax.experimental.pallas import tpu as pltpu
from jax.sharding import PartitionSpec as P

HALO = 64
FREQS = 64
ITERS = 2
STEP_SIZE = 0.05
STEEPNESS = 4.0
THRESHOLD = 1.0
YBLOCK = 64

DIRS = [(di, dj) for di in (0, 1, -1) for dj in (0, 1, -1) if (di, dj) != (0, 0)]


def slot(di, dj):
    return 3 * (di % 3) + dj % 3


def make_tables(core, tile):
    bf16 = jnp.bfloat16
    place = (np.arange(tile) + HALO) % tile
    frequency = np.arange(FREQS) - FREQS // 2

    def waves(position):
        angle = (frequency[None, :] * position[:, None] % tile) * (2.0 * math.pi / tile)
        return np.concatenate([np.cos(angle), np.sin(angle)], 1)

    whole = waves(place).astype(np.float32)
    high = whole.astype(bf16)
    low = (whole - high.astype(np.float32)).astype(bf16)
    below = waves(place - core) * (place >= core)[:, None]
    above = waves(place + core) * (place < 2 * HALO)[:, None]
    spread = np.concatenate([whole, below, above], 1).astype(np.float32)
    return dict(
        forward=np.ascontiguousarray((whole / tile).T).astype(bf16),
        whole=whole,
        half=np.concatenate([high[:core], low[:core], high[:core]], 1),
        inverse_t=np.ascontiguousarray(high[:core].T),
        inverse=high[:core],
        half_t=np.ascontiguousarray(np.concatenate([high[:core], low[:core]], 1).T),
        rows=spread.astype(bf16),
        cols=np.ascontiguousarray((spread / tile).T).astype(bf16),
    )


def kernel(
    axes,
    mask_ref,
    goal_ref,
    kern_ref,
    colour_ref,
    active_ref,
    forward_ref,
    whole_ref,
    half_ref,
    inverse_t_ref,
    inverse_ref,
    half_t_ref,
    rows_ref,
    cols_ref,
    final_ref,
    next_ref,
    mask16,
    vert16,
    side16,
    vert32,
    side32,
    window,
    image,
    grads,
    blocks,
    ka,
    kc,
    goal_t,
    weights,
    halfway,
    d_half,
    send_sems,
    recv_sems,
):
    core = mask_ref.shape[0]
    tile = core + 2 * HALO
    kerns = ka.shape[0]
    f32, bf16 = jnp.float32, jnp.bfloat16
    n_row, n_col = lax.axis_size(axes[0]), lax.axis_size(axes[1])
    row, col = lax.axis_index(axes[0]), lax.axis_index(axes[1])

    def exists(di, dj):
        there = (row + di >= 0) & (row + di < n_row)
        return there & (col + dj >= 0) & (col + dj < n_col)

    barrier = pltpu.get_barrier_semaphore()
    for di, dj in DIRS:

        @pl.when(exists(di, dj))
        def _(di=di, dj=dj):
            pl.semaphore_signal(
                barrier, inc=1, device_id=(row + di, col + dj), device_id_type=pl.DeviceIdType.MESH
            )

    def halo_refs(di, dj, source, vert, side):
        rows = {0: pl.ds(0, core), 1: pl.ds(core - HALO, HALO), -1: pl.ds(0, HALO)}[di]
        if dj == 0:
            return source.at[rows, :], vert.at[1 if di == 1 else 0]
        cols = pl.ds(core - 128, 128) if dj == 1 else pl.ds(0, 128)
        land = {0: pl.ds(0, core), 1: pl.ds(core + HALO, HALO), -1: pl.ds(core, HALO)}[di]
        return source.at[rows, cols], side.at[1 if dj == 1 else 0, land, :]

    def message(phase, di, dj, target):
        if phase < 2:
            pair = (mask16, vert16, side16) if phase == 0 else (mask_ref, vert32, side32)
            source, land = halo_refs(di, dj, *pair)
        else:
            source, land = grads.at[phase - 2, 0], grads.at[phase - 2, slot(-di, -dj)]
        return pltpu.make_async_remote_copy(
            src_ref=source,
            dst_ref=land,
            send_sem=send_sems.at[phase, slot(di, dj)],
            recv_sem=recv_sems.at[phase, slot(di, dj)],
            device_id=target,
            device_id_type=pl.DeviceIdType.MESH,
        )

    def send(phase):
        for di, dj in DIRS:

            @pl.when(exists(di, dj))
            def _(di=di, dj=dj):
                message(phase, di, dj, (row + di, col + dj)).start()

    def wait_arrivals(phase):
        for di, dj in DIRS:

            @pl.when(exists(-di, -dj))
            def _(di=di, dj=dj):
                message(phase, di, dj, (row - di, col - dj)).wait_recv()

    def wait_sent(phase):
        for di, dj in DIRS:

            @pl.when(exists(di, dj))
            def _(di=di, dj=dj):
                message(phase, di, dj, (row + di, col + dj)).wait_send()

    mask16[...] = mask_ref[...].astype(bf16)
    for di, dj in DIRS:

        @pl.when(jnp.logical_not(exists(di, dj)))
        def _(di=di, dj=dj):
            for vert, side in ((vert16, side16), (vert32, side32)):
                _, land = halo_refs(-di, -dj, mask_ref, vert, side)
                land[...] = jnp.zeros(land.shape, land.dtype)
            for step in range(ITERS):
                spot = grads.at[step, slot(di, dj)]
                spot[...] = jnp.zeros(spot.shape, spot.dtype)

    peers = sum(exists(di, dj).astype(jnp.int32) for di, dj in DIRS)
    pl.semaphore_wait(barrier, peers)

    send(0)
    send(1)

    goal_t[...] = goal_ref[...].T
    for k in range(kerns):
        real, imag = kern_ref[k, :FREQS, :], kern_ref[k, FREQS:, :]
        ka[k] = jnp.concatenate([real, -imag], 0).T
        kc[k] = jnp.concatenate([imag, real], 0).T
    update = jnp.where(colour_ref[0, 0] == 0, 1.0, 0.0).astype(f32)
    active = active_ref[0, 0].astype(f32)
    left_half = lax.broadcasted_iota(jnp.int32, (1, 128), 1) < FREQS
    for step in range(ITERS):
        grads[step, 0, FREQS:, :] = jnp.full((16, 128), update, f32).astype(bf16)

    image[:core, :core] = mask16[...]
    window[:core, :core] = mask_ref[...]

    for step in range(ITERS):
        if step == 0:
            wait_arrivals(0)
            image[core : core + HALO, :core] = vert16[0]
            image[core + HALO :, :core] = vert16[1]
            image[:, core:] = jnp.where(
                left_half, side16[0].astype(f32), side16[1].astype(f32)
            ).astype(bf16)
        else:
            image[...] = window[...].astype(bf16)

        partial = lax.dot_general(
            forward_ref[...], image[...], (((1,), (1,)), ((), ())), preferred_element_type=f32
        )
        quads = jnp.dot(
            partial, whole_ref[...], precision=lax.Precision.HIGHEST, preferred_element_type=f32
        ) * (1.0 / tile)
        upper, lower = quads[:FREQS], quads[FREQS:]
        real = upper - pltpu.roll(lower, FREQS, 1)
        imag = -(lower + pltpu.roll(upper, FREQS, 1))
        real = jnp.where(left_half, real, pltpu.roll(real, FREQS, 1))
        imag = jnp.where(left_half, imag, pltpu.roll(imag, FREQS, 1))

        for k in range(kerns):
            x = ka[k] * real - kc[k] * imag
            y = kc[k] * real + ka[k] * imag
            both = jnp.concatenate([jnp.concatenate([x, -y], 0), jnp.concatenate([y, x], 0)], 1)
            high = both.astype(bf16)
            at = pl.ds(k * 256, 256)
            weights[:128, at] = high
            weights[128:256, at] = high
            weights[256:, at] = (both - high.astype(f32)).astype(bf16)
        halfway[...] = jnp.dot(half_ref[...], weights[...], preferred_element_type=f32).astype(bf16)

        def rows_of_y(block, carry):
            at = pl.ds(pl.multiple_of(block * YBLOCK, YBLOCK), YBLOCK)
            stacked = jnp.concatenate(
                [halfway[at, kp * 128 : (kp + 1) * 128] for kp in range(2 * kerns)], 0
            )
            fields = jnp.dot(stacked, inverse_t_ref[...], preferred_element_type=f32)
            fields = fields.reshape(2 * kerns, YBLOCK, core)
            intensity = jnp.sum(fields * fields, axis=0)
            resist = 1.0 / (1.0 + jnp.exp(-STEEPNESS * (intensity - THRESHOLD)))
            slope = (4.0 * STEEPNESS) * (resist - goal_t[at, :]) * (resist * (1.0 - resist))
            d_fields = (fields * slope[None]).astype(bf16).reshape(2 * kerns * YBLOCK, core)
            back = jnp.dot(d_fields, inverse_ref[...], preferred_element_type=f32).astype(bf16)
            for kp in range(2 * kerns):
                d_half[at, kp * 128 : (kp + 1) * 128] = back[kp * YBLOCK : (kp + 1) * YBLOCK]
            return carry

        lax.fori_loop(0, core // YBLOCK, rows_of_y, 0)

        d_weights = jnp.dot(half_t_ref[...], d_half[...], preferred_element_type=f32)
        d_weights = d_weights[:128] + d_weights[128:]
        d_real = jnp.zeros((FREQS, 128), f32)
        d_imag = jnp.zeros((FREQS, 128), f32)
        for k in range(kerns):
            at = k * 256
            dx = d_weights[:FREQS, at : at + 128] + d_weights[FREQS:, at + 128 : at + 256]
            dy = d_weights[:FREQS, at + 128 : at + 256] - d_weights[FREQS:, at : at + 128]
            d_real += ka[k] * dx + kc[k] * dy
            d_imag += ka[k] * dy - kc[k] * dx
        d_real = d_real + pltpu.roll(d_real, FREQS, 1)
        d_imag = d_imag + pltpu.roll(d_imag, FREQS, 1)
        own = jnp.where(left_half, d_real, -d_imag) * (active * (1.0 / tile))
        grads[step, 0, :FREQS, :] = own.astype(bf16)
        send(2 + step)
        if step == 0:
            wait_arrivals(1)
            window[core : core + HALO, :core] = vert32[0]
            window[core + HALO :, :core] = vert32[1]
            window[:, core:] = jnp.where(left_half, side32[0], side32[1])
        wait_arrivals(2 + step)

        for gi in range(3):
            for gj in range(3):
                top = grads[step, 3 * gi + gj, :FREQS, :].astype(f32)
                turned = pltpu.roll(top, FREQS, 1)
                low = jnp.where(left_half, turned, -turned)
                blocks[gj * 128 : gj * 128 + 128, gi * 128 : gi * 128 + 128] = jnp.concatenate(
                    [top, low], 0
                ).astype(bf16)
        spread = lax.dot_general(
            rows_ref[...], blocks[...], (((1,), (1,)), ((), ())), preferred_element_type=f32
        ).astype(bf16)
        total = jnp.dot(spread, cols_ref[...], preferred_element_type=f32)

        bands = ((0, core), (core, HALO), (core + HALO, HALO))
        for gi, (start, size) in enumerate(bands):
            flags = [grads[step, 3 * gi + gj, FREQS : FREQS + 16, :].astype(f32)[:1] for gj in range(3)]
            scale = jnp.concatenate(
                [flags[0]] * (core // 128) + [jnp.where(left_half, flags[1], flags[2])], 1
            )
            at = slice(start, start + size)
            fresh = jnp.clip(window[at, :] - STEP_SIZE * scale * total[at], -1.0, 1.0)
            if step < ITERS - 1:
                window[at, :] = fresh
            else:
                if gi == 0:
                    final_ref[...] = fresh[:, :core]
                out = (start + HALO) % tile
                next_ref[out : out + size, :] = pltpu.roll(fresh, HALO, 1)

    for phase in range(2 + ITERS):
        wait_sent(phase)


def body(axes, mask_field, resist_goal, kernels, colour, active):
    core = mask_field.shape[0]
    tile = core + 2 * HALO
    kerns = kernels.shape[0]
    tables = make_tables(core, tile)
    f32, bf16 = jnp.float32, jnp.bfloat16
    vmem = pl.BlockSpec(memory_space=pltpu.VMEM)
    smem = pl.BlockSpec(memory_space=pltpu.SMEM)
    return pl.pallas_call(
        functools.partial(kernel, axes),
        out_shape=(
            jax.ShapeDtypeStruct((core, core), f32),
            jax.ShapeDtypeStruct((tile, tile), f32),
        ),
        in_specs=[vmem, vmem, vmem, smem, smem] + [vmem] * len(tables),
        out_specs=(vmem, vmem),
        scratch_shapes=[
            pltpu.VMEM((core, core), bf16),
            pltpu.VMEM((2, HALO, core), bf16),
            pltpu.VMEM((2, tile, 128), bf16),
            pltpu.VMEM((2, HALO, core), f32),
            pltpu.VMEM((2, tile, 128), f32),
            pltpu.VMEM((tile, tile), f32),
            pltpu.VMEM((tile, tile), bf16),
            pltpu.VMEM((ITERS, 9, FREQS + 16, 128), bf16),
            pltpu.VMEM((384, 384), bf16),
            pltpu.VMEM((kerns, FREQS, 128), f32),
            pltpu.VMEM((kerns, FREQS, 128), f32),
            pltpu.VMEM((core, core), f32),
            pltpu.VMEM((384, kerns * 256), bf16),
            pltpu.VMEM((core, kerns * 256), bf16),
            pltpu.VMEM((core, kerns * 256), bf16),
            pltpu.SemaphoreType.DMA((2 + ITERS, 9)),
            pltpu.SemaphoreType.DMA((2 + ITERS, 9)),
        ],
        compiler_params=pltpu.CompilerParams(
            collective_id=0, has_side_effects=True, vmem_limit_bytes=48 * 1024 * 1024
        ),
    )(
        mask_field,
        resist_goal,
        kernels.reshape(kerns, 2 * FREQS, FREQS),
        colour,
        active,
        *[jnp.asarray(table) for table in tables.values()],
    )


def solution(mesh):
    axes = mesh.axis_names
    return jax.shard_map(
        functools.partial(body, axes),
        mesh=mesh,
        in_specs=(P(*axes), P(*axes), P(), P(*axes), P(*axes)),
        out_specs=(P(*axes), P(*axes)),
        check_vma=False,
    )
```

profile of v0, /device:TPU:1, one launch (start us, length us, event | category | flops | bytes accessed | tf_op | source)
XLA Modules:
  0.0 48.6 jit_solution(422011224992886657)
XLA Ops:
  1.9 0.0 copy-start
  1.9 1.1 %copy-done = f32[384,384]{1,0:T(8,128)S(1)} copy-done((f32[384,384]{1,0:T(8,128)S(1)}, f32[384,384]{1,0:T(8,128)}, u32[]{:S(2)}) %copy-start) | copy-done | bytes 589848
  3.0 0.0 copy-start.1
  3.0 1.1 %copy-done.1 = f32[384,384]{1,0:T(8,128)S(1)} copy-done((f32[384,384]{1,0:T(8,128)S(1)}, f32[384,384]{1,0:T(8,128)}, u32[]{:S(2)}) %copy-start.1) | copy-done | bytes 589848
  4.1 0.0 copy-start.2
  4.1 1.0 %copy-done.2 = f32[8,2,64,64]{3,2,1,0:T(8,128)S(1)} copy-done((f32[8,2,64,64]{3,2,1,0:T(8,128)S(1)}, f32[8,2,64,64]{3,2,1,0:T(8,128)}, u32[]{:S(2)}) %copy-start.2) | copy-done | bytes 262168
  5.1 0.0 copy-start.3
  5.1 1.0 %copy-done.3 = bf16[384,512]{1,0:T(8,128)(2,1)S(1)} copy-done((bf16[384,512]{1,0:T(8,128)(2,1)S(1)}, bf16[384,512]{1,0:T(8,128)(2,1)}, u32[]{:S(2)}) %copy-start.3) | copy-done | bytes 393240
  6.1 0.0 copy-start.4
  6.1 1.0 %copy-done.4 = bf16[512,384]{1,0:T(8,128)(2,1)S(1)} copy-done((bf16[512,384]{1,0:T(8,128)(2,1)S(1)}, bf16[512,384]{1,0:T(8,128)(2,1)}, u32[]{:S(2)}) %copy-start.4) | copy-done | bytes 393240
  7.1 0.0 copy-start.5
  7.1 1.0 %copy-done.5 = bf16[384,384]{1,0:T(8,128)(2,1)S(1)} copy-done((bf16[384,384]{1,0:T(8,128)(2,1)S(1)}, bf16[384,384]{1,0:T(8,128)(2,1)}, u32[]{:S(2)}) %copy-start.5) | copy-done | bytes 294936
  8.0 0.0 copy-start.6
  8.1 0.9 %copy-done.6 = f32[512,128]{1,0:T(8,128)S(1)} copy-done((f32[512,128]{1,0:T(8,128)S(1)}, f32[512,128]{1,0:T(8,128)}, u32[]{:S(2)}) %copy-start.6) | copy-done | bytes 262168
  9.0 0.0 copy-start.7
  9.0 0.9 %copy-done.7 = bf16[256,384]{1,0:T(8,128)(2,1)S(1)} copy-done((bf16[256,384]{1,0:T(8,128)(2,1)S(1)}, bf16[256,384]{1,0:T(8,128)(2,1)}, u32[]{:S(2)}) %copy-start.7) | copy-done | bytes 196632
  9.9 0.0 copy-start.8
  9.9 0.9 %copy-done.8 = bf16[128,512]{1,0:T(8,128)(2,1)S(1)} copy-done((bf16[128,512]{1,0:T(8,128)(2,1)S(1)}, bf16[128,512]{1,0:T(8,128)(2,1)}, u32[]{:S(2)}) %copy-start.8) | copy-done | bytes 131096
  10.8 0.0 copy-start.9
  10.8 0.9 %copy-done.9 = bf16[384,128]{1,0:T(8,128)(2,1)S(1)} copy-done((bf16[384,128]{1,0:T(8,128)(2,1)S(1)}, bf16[384,128]{1,0:T(8,128)(2,1)}, u32[]{:S(2)}) %copy-start.9) | copy-done | bytes 98328
  11.7 0.0 copy-start.10
  11.7 0.9 %copy-done.10 = bf16[128,384]{1,0:T(8,128)(2,1)S(1)} copy-done((bf16[128,384]{1,0:T(8,128)(2,1)S(1)}, bf16[128,384]{1,0:T(8,128)(2,1)}, u32[]{:S(2)}) %copy-start.10) | copy-done | bytes 98328
  12.6 34.2 %shard_map.140 = (f32[384,384]{1,0:T(8,128)S(1)}, f32[512,512]{1,0:T(8,128)S(1)}) custom-call(f32[384,384]{1,0:T(8,128)S(1)} %copy-done, f32[384,384]{1,0:T(8,128)S(1)} %copy-done.1, f32[8,128,64]{2,1,0:T(8,128)S(1)} %bitcast.1, s32[1,1]{1,0:T(1,128)S(6)} %copy.17.colour_ref, s32[1,1]{1,0:T(1,128)S(6)} %copy.18.active_ref, bf16[128,512]{1,0:T(8,128)(2,1)S(1)} %copy-done.8, ...), custom_call_target="tpu_custom_call" | custom-call | tf_op jit(solution)/shard_map/pallas_call | solution.py:300
  46.8 0.8 %copy.19 = f32[384,384]{1,0:T(8,128)} copy(f32[384,384]{1,0:T(8,128)S(1)} %get-tuple-element.4) | data formatting | bytes 1179648
  47.6 1.0 %copy.20 = f32[512,512]{1,0:T(8,128)} copy(f32[512,512]{1,0:T(8,128)S(1)} %get-tuple-element.5) | data formatting | bytes 2097152
Async XLA Ops:
  1.9 1.1 %copy-start = (f32[384,384]{1,0:T(8,128)S(1)}, f32[384,384]{1,0:T(8,128)}, u32[]{:S(2)}) copy-start(f32[384,384]{1,0:T(8,128)} %mask_ref.1) | copy-start | bytes 1769476
  3.0 1.1 %copy-start.1 = (f32[384,384]{1,0:T(8,128)S(1)}, f32[384,384]{1,0:T(8,128)}, u32[]{:S(2)}) copy-start(f32[384,384]{1,0:T(8,128)} %goal_ref.1) | copy-start | bytes 1769476
  4.1 1.0 %copy-start.2 = (f32[8,2,64,64]{3,2,1,0:T(8,128)S(1)}, f32[8,2,64,64]{3,2,1,0:T(8,128)}, u32[]{:S(2)}) copy-start(f32[8,2,64,64]{3,2,1,0:T(8,128)} %param.15) | copy-start | bytes 786436
  5.1 1.0 %copy-start.3 = (bf16[384,512]{1,0:T(8,128)(2,1)S(1)}, bf16[384,512]{1,0:T(8,128)(2,1)}, u32[]{:S(2)}) copy-start(bf16[384,512]{1,0:T(8,128)(2,1)} %constant.23.clone.cols_ref) | copy-start | bytes 1179652
  6.1 1.0 %copy-start.4 = (bf16[512,384]{1,0:T(8,128)(2,1)S(1)}, bf16[512,384]{1,0:T(8,128)(2,1)}, u32[]{:S(2)}) copy-start(bf16[512,384]{1,0:T(8,128)(2,1)} %constant.22.clone.rows_ref) | copy-start | bytes 1179652
  7.1 1.0 %copy-start.5 = (bf16[384,384]{1,0:T(8,128)(2,1)S(1)}, bf16[384,384]{1,0:T(8,128)(2,1)}, u32[]{:S(2)}) copy-start(bf16[384,384]{1,0:T(8,128)(2,1)} %constant.18.clone.half_ref) | copy-start | bytes 884740
  8.0 0.9 %copy-start.6 = (f32[512,128]{1,0:T(8,128)S(1)}, f32[512,128]{1,0:T(8,128)}, u32[]{:S(2)}) copy-start(f32[512,128]{1,0:T(8,128)} %constant.17.clone.whole_ref) | copy-start | bytes 786436
  9.0 0.9 %copy-start.7 = (bf16[256,384]{1,0:T(8,128)(2,1)S(1)}, bf16[256,384]{1,0:T(8,128)(2,1)}, u32[]{:S(2)}) copy-start(bf16[256,384]{1,0:T(8,128)(2,1)} %constant.21.clone.half_t_ref) | copy-start | bytes 589828
  9.9 0.9 %copy-start.8 = (bf16[128,512]{1,0:T(8,128)(2,1)S(1)}, bf16[128,512]{1,0:T(8,128)(2,1)}, u32[]{:S(2)}) copy-start(bf16[128,512]{1,0:T(8,128)(2,1)} %constant.16.clone.forward_ref) | copy-start | bytes 393220
  10.8 0.9 %copy-start.9 = (bf16[384,128]{1,0:T(8,128)(2,1)S(1)}, bf16[384,128]{1,0:T(8,128)(2,1)}, u32[]{:S(2)}) copy-start(bf16[384,128]{1,0:T(8,128)(2,1)} %constant.20.clone.inverse_ref) | copy-start | bytes 294916
  11.7 0.9 %copy-start.10 = (bf16[128,384]{1,0:T(8,128)(2,1)S(1)}, bf16[128,384]{1,0:T(8,128)(2,1)}, u32[]{:S(2)}) copy-start(bf16[128,384]{1,0:T(8,128)(2,1)} %constant.19.clone.inverse_t_ref) | copy-start | bytes 294916
where the time goes:
time: 49.1 us; the launch traced here: 48.6 us
  Pallas kernels  34.2 us (70%)
  local copies, waits for them, and re-layouts  12.5 us (25%)
  between operations  1.95 us (4%)
    pallas_call x1, Pallas kernels, body(): pl.pallas_call(functools.partial(kernel, axes), out_shape=(jax.ShapeDtype...  34.2 us
    unnamed x24, local copies, waits for them, and re-layouts  12.5 us

commit v1 on v0

--- a/solution.py
+++ b/solution.py
@@ -34,38 +34,53 @@
         return np.concatenate([np.cos(angle), np.sin(angle)], 1)
 
     whole = waves(place).astype(np.float32)
-    high = whole.astype(bf16)
-    low = (whole - high.astype(np.float32)).astype(bf16)
+
+    def split(table):
+        table = table.astype(np.float32)
+        high = table.astype(bf16)
+        return high, (table - high.astype(np.float32)).astype(bf16)
+
     below = waves(place - core) * (place >= core)[:, None]
     above = waves(place + core) * (place < 2 * HALO)[:, None]
     spread = np.concatenate([whole, below, above], 1).astype(np.float32)
+    samples = np.arange(2 * FREQS) * (tile // (2 * FREQS))
+    wave_high, wave_low = split(waves(samples))
+    apart = place[:core, None] - samples[None, :]
+    difference = np.arange(1, FREQS)
+    turns = difference[:, None, None] * apart[None] % tile * (2.0 * math.pi / tile)
+    interpolate = (1.0 + 2.0 * np.cos(turns).sum(0)) / (2 * FREQS)
+    fine_high, fine_low = split(interpolate)
     return dict(
         forward=np.ascontiguousarray((whole / tile).T).astype(bf16),
         whole=whole,
-        half=np.concatenate([high[:core], low[:core], high[:core]], 1),
-        inverse_t=np.ascontiguousarray(high[:core].T),
-        inverse=high[:core],
-        half_t=np.ascontiguousarray(np.concatenate([high[:core], low[:core]], 1).T),
+        half=np.concatenate([wave_high, wave_low, wave_high], 1),
+        inverse_t=np.concatenate([wave_high.T, wave_high.T, wave_low.T], 0),
+        inverse=np.concatenate([wave_high, wave_high], 0),
+        half_t=np.concatenate([wave_high.T, wave_low.T], 1),
+        fine=np.concatenate([fine_high, fine_low, fine_high], 1),
+        fine_t=np.concatenate([fine_high.T, fine_high.T, fine_low.T], 0),
         rows=spread.astype(bf16),
         cols=np.ascontiguousarray((spread / tile).T).astype(bf16),
     )
 
 
-def kernel(
+def halves(value):
+    high = value.astype(jnp.bfloat16)
+    return high, (value - high.astype(jnp.float32)).astype(jnp.bfloat16)
+
+
+def kernel(axes, count, colour_ref, active_ref, *refs):
+    sources, (final_ref, next_ref) = refs[:count], refs[count : count + 2]
+    held = refs[count + 2 : 2 * count + 2]
+    run(axes, colour_ref, active_ref, sources, held, final_ref, next_ref, *refs[2 * count + 2 :])
+
+
+def run(
     axes,
-    mask_ref,
-    goal_ref,
-    kern_ref,
     colour_ref,
     active_ref,
-    forward_ref,
-    whole_ref,
-    half_ref,
-    inverse_t_ref,
-    inverse_ref,
-    half_t_ref,
-    rows_ref,
-    cols_ref,
+    sources,
+    held,
     final_ref,
     next_ref,
     mask16,
@@ -81,11 +96,21 @@
     kc,
     goal_t,
     weights,
-    halfway,
     d_half,
+    intensity,
+    d_intensity,
     send_sems,
     recv_sems,
+    load_sems,
 ):
+    loads = [
+        pltpu.make_async_copy(source, target, load_sems.at[at])
+        for at, (source, target) in enumerate(zip(sources, held))
+    ]
+    for load in loads:
+        load.start()
+    mask_ref, goal_ref, kern_ref, forward_ref, whole_ref, half_ref = held[:6]
+    inverse_t_ref, inverse_ref, half_t_ref, fine_ref, fine_t_ref, rows_ref, cols_ref = held[6:]
     core = mask_ref.shape[0]
     tile = core + 2 * HALO
     kerns = ka.shape[0]
@@ -150,6 +175,7 @@
             def _(di=di, dj=dj):
                 message(phase, di, dj, (row + di, col + dj)).wait_send()
 
+    loads[0].wait()
     mask16[...] = mask_ref[...].astype(bf16)
     for di, dj in DIRS:
 
@@ -168,6 +194,8 @@
     send(0)
     send(1)
 
+    for load in loads[1:]:
+        load.wait()
     goal_t[...] = goal_ref[...].T
     for k in range(kerns):
         real, imag = kern_ref[k, :FREQS, :], kern_ref[k, FREQS:, :]
@@ -214,28 +242,41 @@
             weights[:128, at] = high
             weights[128:256, at] = high
             weights[256:, at] = (both - high.astype(f32)).astype(bf16)
-        halfway[...] = jnp.dot(half_ref[...], weights[...], preferred_element_type=f32).astype(bf16)
-
-        def rows_of_y(block, carry):
-            at = pl.ds(pl.multiple_of(block * YBLOCK, YBLOCK), YBLOCK)
-            stacked = jnp.concatenate(
-                [halfway[at, kp * 128 : (kp + 1) * 128] for kp in range(2 * kerns)], 0
-            )
-            fields = jnp.dot(stacked, inverse_t_ref[...], preferred_element_type=f32)
-            fields = fields.reshape(2 * kerns, YBLOCK, core)
-            intensity = jnp.sum(fields * fields, axis=0)
-            resist = 1.0 / (1.0 + jnp.exp(-STEEPNESS * (intensity - THRESHOLD)))
+        halfway = jnp.dot(half_ref[...], weights[...], preferred_element_type=f32)
+        high, low = halves(halfway)
+        pieces = [slice(kp * 128, (kp + 1) * 128) for kp in range(2 * kerns)]
+        high = jnp.concatenate([high[:, at] for at in pieces], 0)
+        low = jnp.concatenate([low[:, at] for at in pieces], 0)
+        fields = jnp.dot(
+            jnp.concatenate([high, low, high], 1), inverse_t_ref[...], preferred_element_type=f32
+        ).reshape(2 * kerns, 2 * FREQS, 2 * FREQS)
+        high, low = halves(jnp.sum(fields * fields, axis=0))
+        across = jnp.dot(
+            jnp.concatenate([high, low, high], 1), fine_t_ref[...], preferred_element_type=f32
+        )
+        high, low = halves(across)
+        intensity[...] = jnp.dot(
+            fine_ref[...], jnp.concatenate([high, high, low], 0), preferred_element_type=f32
+        )
+        for start in range(0, core, YBLOCK):
+            at = slice(start, start + YBLOCK)
+            resist = 1.0 / (1.0 + jnp.exp(-STEEPNESS * (intensity[at, :] - THRESHOLD)))
             slope = (4.0 * STEEPNESS) * (resist - goal_t[at, :]) * (resist * (1.0 - resist))
-            d_fields = (fields * slope[None]).astype(bf16).reshape(2 * kerns * YBLOCK, core)
-            back = jnp.dot(d_fields, inverse_ref[...], preferred_element_type=f32).astype(bf16)
-            for kp in range(2 * kerns):
-                d_half[at, kp * 128 : (kp + 1) * 128] = back[kp * YBLOCK : (kp + 1) * YBLOCK]
-            return carry
-
-        lax.fori_loop(0, core // YBLOCK, rows_of_y, 0)
+            d_intensity[at, :] = slope.astype(bf16)
+        d_across = jnp.dot(
+            fine_t_ref[: 2 * FREQS, :], d_intensity[...], preferred_element_type=f32
+        ).astype(bf16)
+        d_samples = jnp.dot(d_across, fine_ref[:, : 2 * FREQS], preferred_element_type=f32)
+        high, low = halves((fields * d_samples[None]).reshape(-1, 2 * FREQS))
+        back = jnp.dot(
+            jnp.concatenate([high, low], 1), inverse_ref[...], preferred_element_type=f32
+        ).astype(bf16)
+        for kp, at in enumerate(pieces):
+            piece = back[kp * 128 : (kp + 1) * 128]
+            d_half[:128, at] = piece
+            d_half[128:, at] = piece
 
         d_weights = jnp.dot(half_t_ref[...], d_half[...], preferred_element_type=f32)
-        d_weights = d_weights[:128] + d_weights[128:]
         d_real = jnp.zeros((FREQS, 128), f32)
         d_imag = jnp.zeros((FREQS, 128), f32)
         for k in range(kerns):
@@ -295,17 +336,20 @@
     kerns = kernels.shape[0]
     tables = make_tables(core, tile)
     f32, bf16 = jnp.float32, jnp.bfloat16
+    sources = [mask_field, resist_goal, kernels.reshape(kerns, 2 * FREQS, FREQS)]
+    sources += [jnp.asarray(table) for table in tables.values()]
     vmem = pl.BlockSpec(memory_space=pltpu.VMEM)
     smem = pl.BlockSpec(memory_space=pltpu.SMEM)
     return pl.pallas_call(
-        functools.partial(kernel, axes),
+        functools.partial(kernel, axes, len(sources)),
         out_shape=(
             jax.ShapeDtypeStruct((core, core), f32),
             jax.ShapeDtypeStruct((tile, tile), f32),
         ),
-        in_specs=[vmem, vmem, vmem, smem, smem] + [vmem] * len(tables),
+        in_specs=[smem, smem] + [pl.BlockSpec(memory_space=pltpu.HBM)] * len(sources),
         out_specs=(vmem, vmem),
-        scratch_shapes=[
+        scratch_shapes=[pltpu.VMEM(source.shape, source.dtype) for source in sources]
+        + [
             pltpu.VMEM((core, core), bf16),
             pltpu.VMEM((2, HALO, core), bf16),
             pltpu.VMEM((2, tile, 128), bf16),
@@ -319,21 +363,20 @@
             pltpu.VMEM((kerns, FREQS, 128), f32),
             pltpu.VMEM((core, core), f32),
             pltpu.VMEM((384, kerns * 256), bf16),
-            pltpu.VMEM((core, kerns * 256), bf16),
-            pltpu.VMEM((core, kerns * 256), bf16),
+            pltpu.VMEM((256, kerns * 256), bf16),
+            pltpu.VMEM((core, core), f32),
+            pltpu.VMEM((core, core), bf16),
             pltpu.SemaphoreType.DMA((2 + ITERS, 9)),
             pltpu.SemaphoreType.DMA((2 + ITERS, 9)),
+            pltpu.SemaphoreType.DMA((len(sources),)),
         ],
         compiler_params=pltpu.CompilerParams(
-            collective_id=0, has_side_effects=True, vmem_limit_bytes=48 * 1024 * 1024
+            collective_id=0, has_side_effects=True, vmem_limit_bytes=56 * 1024 * 1024
         ),
     )(
-        mask_field,
-        resist_goal,
-        kernels.reshape(kerns, 2 * FREQS, FREQS),
         colour,
         active,
-        *[jnp.asarray(table) for table in tables.values()],
+        *sources,
     )
 
 

time: 49.1 us -> 32.9 us (0.67)
  local copies, waits for them, and re-layouts: 12.5 us -> 2.98 us
  Pallas kernels: 34.2 us -> 27.8 us
    unnamed x24 -> x4, local copies, waits for them, and re-layouts: 12.5 us -> 2.98 us
    pallas_call x1, Pallas kernels: 34.2 us -> 27.8 us  [body(): pl.pallas_call(functools.partial(kernel, axes, len(sources)), out_shape=(...]
where the time goes in v1:
time: 32.9 us; the launch traced here: 32.7 us
  Pallas kernels  27.8 us (84%)
  local copies, waits for them, and re-layouts  2.98 us (9%)
  between operations  1.94 us (6%)
    pallas_call x1, Pallas kernels, body(): pl.pallas_call(functools.partial(kernel, axes, len(sources)), out_shape=(...  27.8 us
    unnamed x4, local copies, waits for them, and re-layouts  2.98 us

profile of v1, /device:TPU:1, one launch (start us, length us, event | category | flops | bytes accessed | tf_op | source)
XLA Modules:
  0.0 32.7 jit_solution(2623588478321328186)
XLA Ops:
  1.9 27.8 %shard_map.158 = (f32[384,384]{1,0:T(8,128)}, f32[512,512]{1,0:T(8,128)}) custom-call(s32[1,1]{1,0:T(1,128)S(6)} %copy.19.colour_ref, s32[1,1]{1,0:T(1,128)S(6)} %copy.20.active_ref, f32[384,384]{1,0:T(8,128)} %refs_0_.1, f32[384,384]{1,0:T(8,128)} %refs_1_.1, f32[8,128,64]{2,1,0:T(8,128)} %bitcast.1, bf16[128,512]{1,0:T(8,128)(2,1)} %constant.20.clone.refs_3_, ...), custom_call_target="tpu_custom_call" | custom-call | tf_op jit(solution)/shard_map/pallas_call | solution.py:343
  29.7 0.0 copy-start
  29.8 2.0 %copy.21 = f32[384,384]{1,0:T(8,128)} copy(f32[384,384]{1,0:T(8,128)} %get-tuple-element.4) | data formatting | bytes 1179648
  31.8 0.0 copy-done
  31.8 1.0 %copy.22 = f32[512,512]{1,0:T(8,128)} copy(f32[512,512]{1,0:T(8,128)S(1)} %copy-done) | data formatting | bytes 2097152
Async XLA Ops:
  29.7 2.0 %copy-start = (f32[512,512]{1,0:T(8,128)S(1)}, f32[512,512]{1,0:T(8,128)}, u32[]{:S(2)}) copy-start(f32[512,512]{1,0:T(8,128)} %get-tuple-element.5) | copy-start | bytes 3145732

commit v2 on v1

--- a/solution.py
+++ b/solution.py
@@ -17,7 +17,7 @@
 THRESHOLD = 1.0
 YBLOCK = 64
 
-DIRS = [(di, dj) for di in (0, 1, -1) for dj in (0, 1, -1) if (di, dj) != (0, 0)]
+DIRS = [(1, 1), (-1, -1), (1, -1), (-1, 1), (1, 0), (-1, 0), (0, 1), (0, -1)]
 
 
 def slot(di, dj):
@@ -52,7 +52,7 @@
     fine_high, fine_low = split(interpolate)
     return dict(
         forward=np.ascontiguousarray((whole / tile).T).astype(bf16),
-        whole=whole,
+        whole=np.concatenate(split(whole)[:1] * 2 + split(whole)[1:], 0),
         half=np.concatenate([wave_high, wave_low, wave_high], 1),
         inverse_t=np.concatenate([wave_high.T, wave_high.T, wave_low.T], 0),
         inverse=np.concatenate([wave_high, wave_high], 0),
@@ -69,10 +69,75 @@
     return high, (value - high.astype(jnp.float32)).astype(jnp.bfloat16)
 
 
+def bands(core):
+    return ((0, core), (core, HALO), (core + HALO, HALO))
+
+
+def left_lanes():
+    return lax.broadcasted_iota(jnp.int32, (1, 128), 1) < FREQS
+
+
+def band_gradient(slots, blocks, rows_ref, cols_ref):
+    f32, bf16 = jnp.float32, jnp.bfloat16
+    for gi in range(3):
+        for gj in range(3):
+            top = slots[3 * gi + gj, :FREQS, :].astype(f32)
+            turned = pltpu.roll(top, FREQS, 1)
+            low = jnp.where(left_lanes(), turned, -turned)
+            blocks[gj * 128 : gj * 128 + 128, gi * 128 : gi * 128 + 128] = jnp.concatenate(
+                [top, low], 0
+            ).astype(bf16)
+    spread = lax.dot_general(
+        rows_ref[...], blocks[...], (((1,), (1,)), ((), ())), preferred_element_type=f32
+    ).astype(bf16)
+    return jnp.dot(spread, cols_ref[...], preferred_element_type=f32)
+
+
+def flag_row(slots, gi, core):
+    flags = [slots[3 * gi + gj, FREQS : FREQS + 16, :].astype(jnp.float32)[:1] for gj in range(3)]
+    sides = jnp.where(left_lanes(), flags[1], flags[2])
+    return jnp.concatenate([flags[0]] * (core // 128) + [sides], 1)
+
+
+def finish(
+    last_ref, rows_src, cols_src, window_ref, final_ref, next_ref,
+    last, rows, cols, window, blocks, final, following, load_sems, store_sems,
+):
+    loads = [
+        pltpu.make_async_copy(source, target, load_sems.at[at])
+        for at, (source, target) in enumerate(
+            ((last_ref, last), (rows_src, rows), (cols_src, cols), (window_ref, window))
+        )
+    ]
+    for load in loads:
+        load.start()
+    for load in loads:
+        load.wait()
+    core, tile = final.shape[0], following.shape[0]
+    total = band_gradient(last, blocks, rows, cols)
+    stores = []
+    for gi, (start, size) in enumerate(bands(core)):
+        at = slice(start, start + size)
+        scale = flag_row(last, gi, core)
+        fresh = jnp.clip(window[at, :] - STEP_SIZE * scale * total[at], -1.0, 1.0)
+        out = pl.ds((start + HALO) % tile, size)
+        following[out, :] = pltpu.roll(fresh, HALO, 1)
+        stores.append(
+            pltpu.make_async_copy(following.at[out, :], next_ref.at[out, :], store_sems.at[gi])
+        )
+        stores[-1].start()
+        if gi == 0:
+            final[...] = fresh[:, :core]
+            stores.append(pltpu.make_async_copy(final, final_ref, store_sems.at[3]))
+            stores[-1].start()
+    for store in stores:
+        store.wait()
+
+
 def kernel(axes, count, colour_ref, active_ref, *refs):
-    sources, (final_ref, next_ref) = refs[:count], refs[count : count + 2]
+    sources, (window_ref, last_ref) = refs[:count], refs[count : count + 2]
     held = refs[count + 2 : 2 * count + 2]
-    run(axes, colour_ref, active_ref, sources, held, final_ref, next_ref, *refs[2 * count + 2 :])
+    run(axes, colour_ref, active_ref, sources, held, window_ref, last_ref, *refs[2 * count + 2 :])
 
 
 def run(
@@ -81,8 +146,8 @@
     active_ref,
     sources,
     held,
-    final_ref,
-    next_ref,
+    window_ref,
+    last_ref,
     mask16,
     vert16,
     side16,
@@ -102,6 +167,7 @@
     send_sems,
     recv_sems,
     load_sems,
+    keep_sems,
 ):
     loads = [
         pltpu.make_async_copy(source, target, load_sems.at[at])
@@ -139,12 +205,22 @@
         land = {0: pl.ds(0, core), 1: pl.ds(core + HALO, HALO), -1: pl.ds(core, HALO)}[di]
         return source.at[rows, cols], side.at[1 if dj == 1 else 0, land, :]
 
+    def slots_of(step):
+        return last_ref if step == ITERS - 1 else grads.at[step]
+
+    def blank(di, dj):
+        at = slot(di, dj)
+        return pltpu.make_async_copy(grads.at[ITERS - 1, at], last_ref.at[at], keep_sems.at[at])
+
+    keep_own = pltpu.make_async_copy(grads.at[ITERS - 1, 0], last_ref.at[0], keep_sems.at[0])
+    keep_window = pltpu.make_async_copy(window, window_ref, keep_sems.at[9])
+
     def message(phase, di, dj, target):
         if phase < 2:
             pair = (mask16, vert16, side16) if phase == 0 else (mask_ref, vert32, side32)
             source, land = halo_refs(di, dj, *pair)
         else:
-            source, land = grads.at[phase - 2, 0], grads.at[phase - 2, slot(-di, -dj)]
+            source, land = grads.at[phase - 2, 0], slots_of(phase - 2).at[slot(-di, -dj)]
         return pltpu.make_async_remote_copy(
             src_ref=source,
             dst_ref=land,
@@ -187,12 +263,12 @@
             for step in range(ITERS):
                 spot = grads.at[step, slot(di, dj)]
                 spot[...] = jnp.zeros(spot.shape, spot.dtype)
+            blank(di, dj).start()
 
     peers = sum(exists(di, dj).astype(jnp.int32) for di, dj in DIRS)
     pl.semaphore_wait(barrier, peers)
 
     send(0)
-    send(1)
 
     for load in loads[1:]:
         load.wait()
@@ -213,6 +289,7 @@
     for step in range(ITERS):
         if step == 0:
             wait_arrivals(0)
+            send(1)
             image[core : core + HALO, :core] = vert16[0]
             image[core + HALO :, :core] = vert16[1]
             image[:, core:] = jnp.where(
@@ -224,8 +301,9 @@
         partial = lax.dot_general(
             forward_ref[...], image[...], (((1,), (1,)), ((), ())), preferred_element_type=f32
         )
+        high, low = halves(partial)
         quads = jnp.dot(
-            partial, whole_ref[...], precision=lax.Precision.HIGHEST, preferred_element_type=f32
+            jnp.concatenate([high, low, high], 1), whole_ref[...], preferred_element_type=f32
         ) * (1.0 / tile)
         upper, lower = quads[:FREQS], quads[FREQS:]
         real = upper - pltpu.roll(lower, FREQS, 1)
@@ -290,6 +368,9 @@
         own = jnp.where(left_half, d_real, -d_imag) * (active * (1.0 / tile))
         grads[step, 0, :FREQS, :] = own.astype(bf16)
         send(2 + step)
+        if step == ITERS - 1:
+            keep_own.start()
+            keep_window.start()
         if step == 0:
             wait_arrivals(1)
             window[core : core + HALO, :core] = vert32[0]
@@ -297,34 +378,19 @@
             window[:, core:] = jnp.where(left_half, side32[0], side32[1])
         wait_arrivals(2 + step)
 
-        for gi in range(3):
-            for gj in range(3):
-                top = grads[step, 3 * gi + gj, :FREQS, :].astype(f32)
-                turned = pltpu.roll(top, FREQS, 1)
-                low = jnp.where(left_half, turned, -turned)
-                blocks[gj * 128 : gj * 128 + 128, gi * 128 : gi * 128 + 128] = jnp.concatenate(
-                    [top, low], 0
-                ).astype(bf16)
-        spread = lax.dot_general(
-            rows_ref[...], blocks[...], (((1,), (1,)), ((), ())), preferred_element_type=f32
-        ).astype(bf16)
-        total = jnp.dot(spread, cols_ref[...], preferred_element_type=f32)
-
-        bands = ((0, core), (core, HALO), (core + HALO, HALO))
-        for gi, (start, size) in enumerate(bands):
-            flags = [grads[step, 3 * gi + gj, FREQS : FREQS + 16, :].astype(f32)[:1] for gj in range(3)]
-            scale = jnp.concatenate(
-                [flags[0]] * (core // 128) + [jnp.where(left_half, flags[1], flags[2])], 1
-            )
-            at = slice(start, start + size)
-            fresh = jnp.clip(window[at, :] - STEP_SIZE * scale * total[at], -1.0, 1.0)
-            if step < ITERS - 1:
-                window[at, :] = fresh
-            else:
-                if gi == 0:
-                    final_ref[...] = fresh[:, :core]
-                out = (start + HALO) % tile
-                next_ref[out : out + size, :] = pltpu.roll(fresh, HALO, 1)
+        if step < ITERS - 1:
+            total = band_gradient(grads.at[step], blocks, rows_ref, cols_ref)
+            for gi, (start, size) in enumerate(bands(core)):
+                at = slice(start, start + size)
+                scale = flag_row(grads.at[step], gi, core)
+                window[at, :] = jnp.clip(window[at, :] - STEP_SIZE * scale * total[at], -1.0, 1.0)
+    keep_window.wait()
+    keep_own.wait()
+    for di, dj in DIRS:
+
+        @pl.when(jnp.logical_not(exists(di, dj)))
+        def _(di=di, dj=dj):
+            blank(di, dj).wait()
 
     for phase in range(2 + ITERS):
         wait_sent(phase)
@@ -338,16 +404,16 @@
     f32, bf16 = jnp.float32, jnp.bfloat16
     sources = [mask_field, resist_goal, kernels.reshape(kerns, 2 * FREQS, FREQS)]
     sources += [jnp.asarray(table) for table in tables.values()]
-    vmem = pl.BlockSpec(memory_space=pltpu.VMEM)
+    hbm = pl.BlockSpec(memory_space=pltpu.HBM)
     smem = pl.BlockSpec(memory_space=pltpu.SMEM)
-    return pl.pallas_call(
+    window, last = pl.pallas_call(
         functools.partial(kernel, axes, len(sources)),
         out_shape=(
-            jax.ShapeDtypeStruct((core, core), f32),
             jax.ShapeDtypeStruct((tile, tile), f32),
+            jax.ShapeDtypeStruct((9, FREQS + 16, 128), bf16),
         ),
-        in_specs=[smem, smem] + [pl.BlockSpec(memory_space=pltpu.HBM)] * len(sources),
-        out_specs=(vmem, vmem),
+        in_specs=[smem, smem] + [hbm] * len(sources),
+        out_specs=(hbm, hbm),
         scratch_shapes=[pltpu.VMEM(source.shape, source.dtype) for source in sources]
         + [
             pltpu.VMEM((core, core), bf16),
@@ -369,6 +435,7 @@
             pltpu.SemaphoreType.DMA((2 + ITERS, 9)),
             pltpu.SemaphoreType.DMA((2 + ITERS, 9)),
             pltpu.SemaphoreType.DMA((len(sources),)),
+            pltpu.SemaphoreType.DMA((10,)),
         ],
         compiler_params=pltpu.CompilerParams(
             collective_id=0, has_side_effects=True, vmem_limit_bytes=56 * 1024 * 1024
@@ -378,6 +445,25 @@
         active,
         *sources,
     )
+    finals = [last, sources[-2], sources[-1], window]
+    return pl.pallas_call(
+        finish,
+        out_shape=(
+            jax.ShapeDtypeStruct((core, core), f32),
+            jax.ShapeDtypeStruct((tile, tile), f32),
+        ),
+        in_specs=[hbm] * len(finals),
+        out_specs=(hbm, hbm),
+        scratch_shapes=[pltpu.VMEM(source.shape, source.dtype) for source in finals]
+        + [
+            pltpu.VMEM((384, 384), bf16),
+            pltpu.VMEM((core, core), f32),
+            pltpu.VMEM((tile, tile), f32),
+            pltpu.SemaphoreType.DMA((4,)),
+            pltpu.SemaphoreType.DMA((4,)),
+        ],
+        compiler_params=pltpu.CompilerParams(vmem_limit_bytes=56 * 1024 * 1024),
+    )(*finals)
 
 
 def solution(mesh):

time: 32.9 us -> 31.7 us (0.964)
  the two profiles are of different devices: /device:TPU:1 before, /device:TPU:3 now
where the time goes in v2:
time: 31.7 us; the launch traced here: 31.5 us
  Pallas kernels  29.6 us (93%)
  between operations  1.93 us (6%)
    pallas_call x1, Pallas kernels, body(): pl.pallas_call(functools.partial(kernel, axes, len(sources)), out_shape=(...  25.8 us
    pallas_call x1, Pallas kernels, body(): pl.pallas_call(finish, out_shape=(jax.ShapeDtypeStruct((core, core), f32)...  3.75 us

profile of v2, /device:TPU:3, one launch (start us, length us, event | category | flops | bytes accessed | tf_op | source)
XLA Modules:
  0.0 31.5 jit_solution(4996051742746887386)
XLA Ops:
  1.9 25.8 %shard_map.158 = (f32[512,512]{1,0:T(8,128)}, bf16[9,80,128]{2,1,0:T(8,128)(2,1)}) custom-call(s32[1,1]{1,0:T(1,128)S(6)} %copy.17.colour_ref, s32[1,1]{1,0:T(1,128)S(6)} %copy.18.active_ref, f32[384,384]{1,0:T(8,128)} %refs_0_.1, f32[384,384]{1,0:T(8,128)} %refs_1_.1, f32[8,128,64]{2,1,0:T(8,128)} %bitcast.1, bf16[128,512]{1,0:T(8,128)(2,1)} %constant.20.clone.refs_3_, ...), custom_call_target="tpu_custom_call" | custom-call | tf_op jit(solution)/shard_map/pallas_call | solution.py:409
  27.8 3.8 %shard_map.159 = (f32[384,384]{1,0:T(8,128)}, f32[512,512]{1,0:T(8,128)}) custom-call(bf16[9,80,128]{2,1,0:T(8,128)(2,1)} %get-tuple-element.4.last_ref, bf16[512,384]{1,0:T(8,128)(2,1)} %constant.28.clone.refs_11_.rows_src, bf16[384,512]{1,0:T(8,128)(2,1)} %constant.29.clone.refs_12_.cols_src, f32[512,512]{1,0:T(8,128)} %get-tuple-element.5.window_ref), custom_call_target="tpu_custom_call" | custom-call | tf_op jit(solution)/shard_map/pallas_call | solution.py:449

commit v3 on v2

--- a/solution.py
+++ b/solution.py
@@ -16,6 +16,7 @@
 STEEPNESS = 4.0
 THRESHOLD = 1.0
 YBLOCK = 64
+FLAG_LANE = FREQS + FREQS // 2
 
 DIRS = [(1, 1), (-1, -1), (1, -1), (-1, 1), (1, 0), (-1, 0), (0, 1), (0, -1)]
 
@@ -53,9 +54,9 @@
     return dict(
         forward=np.ascontiguousarray((whole / tile).T).astype(bf16),
         whole=np.concatenate(split(whole)[:1] * 2 + split(whole)[1:], 0),
-        half=np.concatenate([wave_high, wave_low, wave_high], 1),
-        inverse_t=np.concatenate([wave_high.T, wave_high.T, wave_low.T], 0),
-        inverse=np.concatenate([wave_high, wave_high], 0),
+        half=np.concatenate([wave_high, wave_low], 1),
+        inverse_t=np.concatenate([wave_high.T, wave_low.T], 0),
+        inverse=wave_high,
         half_t=np.concatenate([wave_high.T, wave_low.T], 1),
         fine=np.concatenate([fine_high, fine_low, fine_high], 1),
         fine_t=np.concatenate([fine_high.T, fine_high.T, fine_low.T], 0),
@@ -69,6 +70,10 @@
     return high, (value - high.astype(jnp.float32)).astype(jnp.bfloat16)
 
 
+def whole_of(high, low):
+    return high.astype(jnp.float32) + low.astype(jnp.float32)
+
+
 def bands(core):
     return ((0, core), (core, HALO), (core + HALO, HALO))
 
@@ -77,16 +82,18 @@
     return lax.broadcasted_iota(jnp.int32, (1, 128), 1) < FREQS
 
 
-def band_gradient(slots, blocks, rows_ref, cols_ref):
+def band_gradient(slots, blocks, rows_ref, cols_ref, loads=()):
     f32, bf16 = jnp.float32, jnp.bfloat16
     for gi in range(3):
         for gj in range(3):
-            top = slots[3 * gi + gj, :FREQS, :].astype(f32)
+            top = slots[3 * gi + gj].astype(f32)
             turned = pltpu.roll(top, FREQS, 1)
             low = jnp.where(left_lanes(), turned, -turned)
             blocks[gj * 128 : gj * 128 + 128, gi * 128 : gi * 128 + 128] = jnp.concatenate(
                 [top, low], 0
             ).astype(bf16)
+    for load in loads:
+        load.wait()
     spread = lax.dot_general(
         rows_ref[...], blocks[...], (((1,), (1,)), ((), ())), preferred_element_type=f32
     ).astype(bf16)
@@ -94,7 +101,11 @@
 
 
 def flag_row(slots, gi, core):
-    flags = [slots[3 * gi + gj, FREQS : FREQS + 16, :].astype(jnp.float32)[:1] for gj in range(3)]
+    at = FREQS // 2
+    here = lax.broadcasted_iota(jnp.int32, (1, 128), 1) == FLAG_LANE
+    flags = [slots[3 * gi + gj, at : at + 16, :].astype(jnp.float32)[:1] for gj in range(3)]
+    flags = [jnp.sum(jnp.where(here, flag, 0.0), axis=1, keepdims=True) for flag in flags]
+    flags = [jnp.broadcast_to(flag, (1, 128)) for flag in flags]
     sides = jnp.where(left_lanes(), flags[1], flags[2])
     return jnp.concatenate([flags[0]] * (core // 128) + [sides], 1)
 
@@ -111,10 +122,10 @@
     ]
     for load in loads:
         load.start()
-    for load in loads:
-        load.wait()
     core, tile = final.shape[0], following.shape[0]
-    total = band_gradient(last, blocks, rows, cols)
+    loads[0].wait()
+    total = band_gradient(last, blocks, rows, cols, loads[1:3])
+    loads[3].wait()
     stores = []
     for gi, (start, size) in enumerate(bands(core)):
         at = slice(start, start + size)
@@ -149,10 +160,11 @@
     window_ref,
     last_ref,
     mask16,
+    rest16,
     vert16,
     side16,
-    vert32,
-    side32,
+    vert_rest,
+    side_rest,
     window,
     image,
     grads,
@@ -173,8 +185,7 @@
         pltpu.make_async_copy(source, target, load_sems.at[at])
         for at, (source, target) in enumerate(zip(sources, held))
     ]
-    for load in loads:
-        load.start()
+    loads[0].start()
     mask_ref, goal_ref, kern_ref, forward_ref, whole_ref, half_ref = held[:6]
     inverse_t_ref, inverse_ref, half_t_ref, fine_ref, fine_t_ref, rows_ref, cols_ref = held[6:]
     core = mask_ref.shape[0]
@@ -217,7 +228,7 @@
 
     def message(phase, di, dj, target):
         if phase < 2:
-            pair = (mask16, vert16, side16) if phase == 0 else (mask_ref, vert32, side32)
+            pair = (mask16, vert16, side16) if phase == 0 else (rest16, vert_rest, side_rest)
             source, land = halo_refs(di, dj, *pair)
         else:
             source, land = grads.at[phase - 2, 0], slots_of(phase - 2).at[slot(-di, -dj)]
@@ -252,12 +263,14 @@
                 message(phase, di, dj, (row + di, col + dj)).wait_send()
 
     loads[0].wait()
-    mask16[...] = mask_ref[...].astype(bf16)
+    for load in loads[1:]:
+        load.start()
+    mask16[...], rest16[...] = halves(mask_ref[...])
     for di, dj in DIRS:
 
         @pl.when(jnp.logical_not(exists(di, dj)))
         def _(di=di, dj=dj):
-            for vert, side in ((vert16, side16), (vert32, side32)):
+            for vert, side in ((vert16, side16), (vert_rest, side_rest)):
                 _, land = halo_refs(-di, -dj, mask_ref, vert, side)
                 land[...] = jnp.zeros(land.shape, land.dtype)
             for step in range(ITERS):
@@ -280,8 +293,8 @@
     update = jnp.where(colour_ref[0, 0] == 0, 1.0, 0.0).astype(f32)
     active = active_ref[0, 0].astype(f32)
     left_half = lax.broadcasted_iota(jnp.int32, (1, 128), 1) < FREQS
-    for step in range(ITERS):
-        grads[step, 0, FREQS:, :] = jnp.full((16, 128), update, f32).astype(bf16)
+    flag_spot = lax.broadcasted_iota(jnp.int32, (FREQS, 128), 0) == FREQS // 2
+    flag_spot &= lax.broadcasted_iota(jnp.int32, (FREQS, 128), 1) == FLAG_LANE
 
     image[:core, :core] = mask16[...]
     window[:core, :core] = mask_ref[...]
@@ -318,15 +331,12 @@
             high = both.astype(bf16)
             at = pl.ds(k * 256, 256)
             weights[:128, at] = high
-            weights[128:256, at] = high
-            weights[256:, at] = (both - high.astype(f32)).astype(bf16)
-        halfway = jnp.dot(half_ref[...], weights[...], preferred_element_type=f32)
-        high, low = halves(halfway)
+            weights[128:, at] = high
+        halfway = jnp.dot(half_ref[...], weights[...], preferred_element_type=f32).astype(bf16)
         pieces = [slice(kp * 128, (kp + 1) * 128) for kp in range(2 * kerns)]
-        high = jnp.concatenate([high[:, at] for at in pieces], 0)
-        low = jnp.concatenate([low[:, at] for at in pieces], 0)
+        stacked = jnp.concatenate([halfway[:, at] for at in pieces], 0)
         fields = jnp.dot(
-            jnp.concatenate([high, low, high], 1), inverse_t_ref[...], preferred_element_type=f32
+            jnp.concatenate([stacked, stacked], 1), inverse_t_ref[...], preferred_element_type=f32
         ).reshape(2 * kerns, 2 * FREQS, 2 * FREQS)
         high, low = halves(jnp.sum(fields * fields, axis=0))
         across = jnp.dot(
@@ -345,10 +355,8 @@
             fine_t_ref[: 2 * FREQS, :], d_intensity[...], preferred_element_type=f32
         ).astype(bf16)
         d_samples = jnp.dot(d_across, fine_ref[:, : 2 * FREQS], preferred_element_type=f32)
-        high, low = halves((fields * d_samples[None]).reshape(-1, 2 * FREQS))
-        back = jnp.dot(
-            jnp.concatenate([high, low], 1), inverse_ref[...], preferred_element_type=f32
-        ).astype(bf16)
+        d_fields = (fields * d_samples[None]).astype(bf16).reshape(-1, 2 * FREQS)
+        back = jnp.dot(d_fields, inverse_ref[...], preferred_element_type=f32).astype(bf16)
         for kp, at in enumerate(pieces):
             piece = back[kp * 128 : (kp + 1) * 128]
             d_half[:128, at] = piece
@@ -366,16 +374,19 @@
         d_real = d_real + pltpu.roll(d_real, FREQS, 1)
         d_imag = d_imag + pltpu.roll(d_imag, FREQS, 1)
         own = jnp.where(left_half, d_real, -d_imag) * (active * (1.0 / tile))
-        grads[step, 0, :FREQS, :] = own.astype(bf16)
+        grads[step, 0] = jnp.where(flag_spot, update, own).astype(bf16)
         send(2 + step)
         if step == ITERS - 1:
             keep_own.start()
             keep_window.start()
         if step == 0:
             wait_arrivals(1)
-            window[core : core + HALO, :core] = vert32[0]
-            window[core + HALO :, :core] = vert32[1]
-            window[:, core:] = jnp.where(left_half, side32[0], side32[1])
+            for at in (0, 1):
+                start = core + at * HALO
+                window[start : start + HALO, :core] = whole_of(vert16[at], vert_rest[at])
+            window[:, core:] = jnp.where(
+                left_half, whole_of(side16[0], side_rest[0]), whole_of(side16[1], side_rest[1])
+            )
         wait_arrivals(2 + step)
 
         if step < ITERS - 1:
@@ -410,25 +421,26 @@
         functools.partial(kernel, axes, len(sources)),
         out_shape=(
             jax.ShapeDtypeStruct((tile, tile), f32),
-            jax.ShapeDtypeStruct((9, FREQS + 16, 128), bf16),
+            jax.ShapeDtypeStruct((9, FREQS, 128), bf16),
         ),
         in_specs=[smem, smem] + [hbm] * len(sources),
         out_specs=(hbm, hbm),
         scratch_shapes=[pltpu.VMEM(source.shape, source.dtype) for source in sources]
         + [
             pltpu.VMEM((core, core), bf16),
+            pltpu.VMEM((core, core), bf16),
             pltpu.VMEM((2, HALO, core), bf16),
             pltpu.VMEM((2, tile, 128), bf16),
-            pltpu.VMEM((2, HALO, core), f32),
-            pltpu.VMEM((2, tile, 128), f32),
+            pltpu.VMEM((2, HALO, core), bf16),
+            pltpu.VMEM((2, tile, 128), bf16),
             pltpu.VMEM((tile, tile), f32),
             pltpu.VMEM((tile, tile), bf16),
-            pltpu.VMEM((ITERS, 9, FREQS + 16, 128), bf16),
+            pltpu.VMEM((ITERS, 9, FREQS, 128), bf16),
             pltpu.VMEM((384, 384), bf16),
             pltpu.VMEM((kerns, FREQS, 128), f32),
             pltpu.VMEM((kerns, FREQS, 128), f32),
             pltpu.VMEM((core, core), f32),
-            pltpu.VMEM((384, kerns * 256), bf16),
+            pltpu.VMEM((256, kerns * 256), bf16),
             pltpu.VMEM((256, kerns * 256), bf16),
             pltpu.VMEM((core, core), f32),
             pltpu.VMEM((core, core), bf16),

time: 31.7 us -> 29.3 us (0.924)
  the two profiles are of different devices: /device:TPU:3 before, /device:TPU:1 now
where the time goes in v3:
time: 29.3 us; the launch traced here: 28.9 us
  Pallas kernels  26.9 us (92%)
  between operations  1.93 us (7%)
    pallas_call x1, Pallas kernels, body(): pl.pallas_call(functools.partial(kernel, axes, len(sources)), out_shape=(...  23.4 us
    pallas_call x1, Pallas kernels, body(): pl.pallas_call(finish, out_shape=(jax.ShapeDtypeStruct((core, core), f32)...  3.54 us

profile of v3, /device:TPU:1, one launch (start us, length us, event | category | flops | bytes accessed | tf_op | source)
XLA Modules:
  0.0 28.9 jit_solution(3335164938846825145)
XLA Ops:
  1.9 23.4 %shard_map.158 = (f32[512,512]{1,0:T(8,128)}, bf16[9,64,128]{2,1,0:T(8,128)(2,1)}) custom-call(s32[1,1]{1,0:T(1,128)S(6)} %copy.17.colour_ref, s32[1,1]{1,0:T(1,128)S(6)} %copy.18.active_ref, f32[384,384]{1,0:T(8,128)} %refs_0_.1, f32[384,384]{1,0:T(8,128)} %refs_1_.1, f32[8,128,64]{2,1,0:T(8,128)} %bitcast.1, bf16[128,512]{1,0:T(8,128)(2,1)} %constant.20.clone.refs_3_, ...), custom_call_target="tpu_custom_call" | custom-call | tf_op jit(solution)/shard_map/pallas_call | solution.py:420
  25.3 3.5 %shard_map.159 = (f32[384,384]{1,0:T(8,128)}, f32[512,512]{1,0:T(8,128)}) custom-call(bf16[9,64,128]{2,1,0:T(8,128)(2,1)} %get-tuple-element.4.last_ref, bf16[512,384]{1,0:T(8,128)(2,1)} %constant.28.clone.refs_11_.rows_src, bf16[384,512]{1,0:T(8,128)(2,1)} %constant.29.clone.refs_12_.cols_src, f32[512,512]{1,0:T(8,128)} %get-tuple-element.5.window_ref), custom_call_target="tpu_custom_call" | custom-call | tf_op jit(solution)/shard_map/pallas_call | solution.py:461

commit v4 on v3

--- a/solution.py
+++ b/solution.py
@@ -74,6 +74,25 @@
     return high.astype(jnp.float32) + low.astype(jnp.float32)
 
 
+def pack_side(block, right):
+    half = block.shape[0] // 2
+    upper, lower = block[:half], block[half:]
+    if right:
+        return jnp.where(left_lanes(), pltpu.roll(upper, FREQS, 1), lower)
+    return jnp.where(left_lanes(), upper, pltpu.roll(lower, FREQS, 1))
+
+
+def join_sides(from_right, from_left):
+    upper = jnp.where(left_lanes(), from_right, pltpu.roll(from_left, FREQS, 1))
+    lower = jnp.where(left_lanes(), pltpu.roll(from_right, FREQS, 1), from_left)
+    return jnp.concatenate([upper, lower], 0)
+
+
+def side_parts(core):
+    whole, corner = core // 2, HALO // 2
+    return {0: (0, whole), -1: (whole, corner), 1: (whole + corner, corner)}
+
+
 def bands(core):
     return ((0, core), (core, HALO), (core + HALO, HALO))
 
@@ -161,6 +180,8 @@
     last_ref,
     mask16,
     rest16,
+    pack16,
+    pack_rest,
     vert16,
     side16,
     vert_rest,
@@ -208,13 +229,15 @@
                 barrier, inc=1, device_id=(row + di, col + dj), device_id_type=pl.DeviceIdType.MESH
             )
 
-    def halo_refs(di, dj, source, vert, side):
-        rows = {0: pl.ds(0, core), 1: pl.ds(core - HALO, HALO), -1: pl.ds(0, HALO)}[di]
+    first = (mask16, pack16, vert16, side16)
+    second = (rest16, pack_rest, vert_rest, side_rest)
+
+    def halo_refs(di, dj, source, packed, vert, side):
         if dj == 0:
+            rows = pl.ds(core - HALO, HALO) if di == 1 else pl.ds(0, HALO)
             return source.at[rows, :], vert.at[1 if di == 1 else 0]
-        cols = pl.ds(core - 128, 128) if dj == 1 else pl.ds(0, 128)
-        land = {0: pl.ds(0, core), 1: pl.ds(core + HALO, HALO), -1: pl.ds(core, HALO)}[di]
-        return source.at[rows, cols], side.at[1 if dj == 1 else 0, land, :]
+        at = pl.ds(*side_parts(core)[di])
+        return packed.at[1 if dj == 1 else 0, at, :], side.at[1 if dj == 1 else 0, at, :]
 
     def slots_of(step):
         return last_ref if step == ITERS - 1 else grads.at[step]
@@ -228,7 +251,7 @@
 
     def message(phase, di, dj, target):
         if phase < 2:
-            pair = (mask16, vert16, side16) if phase == 0 else (rest16, vert_rest, side_rest)
+            pair = first if phase == 0 else second
             source, land = halo_refs(di, dj, *pair)
         else:
             source, land = grads.at[phase - 2, 0], slots_of(phase - 2).at[slot(-di, -dj)]
@@ -265,13 +288,28 @@
     loads[0].wait()
     for load in loads[1:]:
         load.start()
-    mask16[...], rest16[...] = halves(mask_ref[...])
+    def pack(source, packed):
+        for right in (0, 1):
+            lanes = slice(core - 128, core) if right else slice(0, 128)
+            for di, rows in ((0, slice(0, core)), (-1, slice(0, HALO)), (1, slice(core - HALO, core))):
+                start, size = side_parts(core)[di]
+                part = pack_side(source[rows, lanes].astype(f32), right)
+                packed[right, start : start + size, :] = part.astype(bf16)
+
+    def unpack(side):
+        parts = [side_parts(core)[di] for di in (0, -1, 1)]
+        return jnp.concatenate(
+            [join_sides(*[side[at, p : p + n, :].astype(f32) for at in (0, 1)]) for p, n in parts], 0
+        )
+
+    mask16[...] = mask_ref[...].astype(bf16)
+    pack(mask16, pack16)
     for di, dj in DIRS:
 
         @pl.when(jnp.logical_not(exists(di, dj)))
         def _(di=di, dj=dj):
-            for vert, side in ((vert16, side16), (vert_rest, side_rest)):
-                _, land = halo_refs(-di, -dj, mask_ref, vert, side)
+            for pair in (first, second):
+                _, land = halo_refs(-di, -dj, *pair)
                 land[...] = jnp.zeros(land.shape, land.dtype)
             for step in range(ITERS):
                 spot = grads.at[step, slot(di, dj)]
@@ -282,6 +320,8 @@
     pl.semaphore_wait(barrier, peers)
 
     send(0)
+    rest16[...] = (mask_ref[...] - mask16[...].astype(f32)).astype(bf16)
+    pack(rest16, pack_rest)
 
     for load in loads[1:]:
         load.wait()
@@ -305,9 +345,7 @@
             send(1)
             image[core : core + HALO, :core] = vert16[0]
             image[core + HALO :, :core] = vert16[1]
-            image[:, core:] = jnp.where(
-                left_half, side16[0].astype(f32), side16[1].astype(f32)
-            ).astype(bf16)
+            image[:, core:] = unpack(side16).astype(bf16)
         else:
             image[...] = window[...].astype(bf16)
 
@@ -384,9 +422,7 @@
             for at in (0, 1):
                 start = core + at * HALO
                 window[start : start + HALO, :core] = whole_of(vert16[at], vert_rest[at])
-            window[:, core:] = jnp.where(
-                left_half, whole_of(side16[0], side_rest[0]), whole_of(side16[1], side_rest[1])
-            )
+            window[:, core:] = unpack(side16) + unpack(side_rest)
         wait_arrivals(2 + step)
 
         if step < ITERS - 1:
@@ -429,10 +465,12 @@
         + [
             pltpu.VMEM((core, core), bf16),
             pltpu.VMEM((core, core), bf16),
+            pltpu.VMEM((2, tile // 2, 128), bf16),
+            pltpu.VMEM((2, tile // 2, 128), bf16),
             pltpu.VMEM((2, HALO, core), bf16),
-            pltpu.VMEM((2, tile, 128), bf16),
+            pltpu.VMEM((2, tile // 2, 128), bf16),
             pltpu.VMEM((2, HALO, core), bf16),
-            pltpu.VMEM((2, tile, 128), bf16),
+            pltpu.VMEM((2, tile // 2, 128), bf16),
             pltpu.VMEM((tile, tile), f32),
             pltpu.VMEM((tile, tile), bf16),
             pltpu.VMEM((ITERS, 9, FREQS, 128), bf16),

time: 29.3 us -> 28.7 us (0.980)
  Pallas kernels: 26.9 us -> 26.6 us
    pallas_call x1, Pallas kernels: 23.4 us -> 23 us  [body(): pl.pallas_call(functools.partial(kernel, axes, len(sources)), out_shape=(...]
where the time goes in v4:
time: 28.7 us; the launch traced here: 28.5 us
  Pallas kernels  26.6 us (93%)
  between operations  1.93 us (7%)
    pallas_call x1, Pallas kernels, body(): pl.pallas_call(functools.partial(kernel, axes, len(sources)), out_shape=(...  23 us
    pallas_call x1, Pallas kernels, body(): pl.pallas_call(finish, out_shape=(jax.ShapeDtypeStruct((core, core), f32)...  3.54 us

profile of v4, /device:TPU:1, one launch (start us, length us, event | category | flops | bytes accessed | tf_op | source)
XLA Modules:
  0.0 28.5 jit_solution(4389906217231314890)
XLA Ops:
  1.9 23.0 %shard_map.158 = (f32[512,512]{1,0:T(8,128)}, bf16[9,64,128]{2,1,0:T(8,128)(2,1)}) custom-call(s32[1,1]{1,0:T(1,128)S(6)} %copy.17.colour_ref, s32[1,1]{1,0:T(1,128)S(6)} %copy.18.active_ref, f32[384,384]{1,0:T(8,128)} %refs_0_.1, f32[384,384]{1,0:T(8,128)} %refs_1_.1, f32[8,128,64]{2,1,0:T(8,128)} %bitcast.1, bf16[128,512]{1,0:T(8,128)(2,1)} %constant.20.clone.refs_3_, ...), custom_call_target="tpu_custom_call" | custom-call | tf_op jit(solution)/shard_map/pallas_call | solution.py:456
  25.0 3.5 %shard_map.159 = (f32[384,384]{1,0:T(8,128)}, f32[512,512]{1,0:T(8,128)}) custom-call(bf16[9,64,128]{2,1,0:T(8,128)(2,1)} %get-tuple-element.4.last_ref, bf16[512,384]{1,0:T(8,128)(2,1)} %constant.28.clone.refs_11_.rows_src, bf16[384,512]{1,0:T(8,128)(2,1)} %constant.29.clone.refs_12_.cols_src, f32[512,512]{1,0:T(8,128)} %get-tuple-element.5.window_ref), custom_call_target="tpu_custom_call" | custom-call | tf_op jit(solution)/shard_map/pallas_call | solution.py:499

commit v5 on v4

--- a/solution.py
+++ b/solution.py
@@ -101,7 +101,7 @@
     return lax.broadcasted_iota(jnp.int32, (1, 128), 1) < FREQS
 
 
-def band_gradient(slots, blocks, rows_ref, cols_ref, loads=()):
+def band_gradient(slots, blocks, rows_ref, loads=()):
     f32, bf16 = jnp.float32, jnp.bfloat16
     for gi in range(3):
         for gj in range(3):
@@ -116,7 +116,7 @@
     spread = lax.dot_general(
         rows_ref[...], blocks[...], (((1,), (1,)), ((), ())), preferred_element_type=f32
     ).astype(bf16)
-    return jnp.dot(spread, cols_ref[...], preferred_element_type=f32)
+    return spread
 
 
 def flag_row(slots, gi, core):
@@ -143,13 +143,18 @@
         load.start()
     core, tile = final.shape[0], following.shape[0]
     loads[0].wait()
-    total = band_gradient(last, blocks, rows, cols, loads[1:3])
+    spread = band_gradient(last, blocks, rows, loads[1:2])
+    loads[2].wait()
     loads[3].wait()
     stores = []
     for gi, (start, size) in enumerate(bands(core)):
         at = slice(start, start + size)
         scale = flag_row(last, gi, core)
-        fresh = jnp.clip(window[at, :] - STEP_SIZE * scale * total[at], -1.0, 1.0)
+        if gi < 2:
+            below = slice(0, core) if gi == 0 else slice(core, tile)
+            part = jnp.dot(spread[below], cols[...], preferred_element_type=jnp.float32)
+        total = part if gi == 0 else part[start - core : start - core + size]
+        fresh = jnp.clip(window[at, :] - STEP_SIZE * scale * total, -1.0, 1.0)
         out = pl.ds((start + HALO) % tile, size)
         following[out, :] = pltpu.roll(fresh, HALO, 1)
         stores.append(
@@ -417,6 +422,15 @@
         if step == ITERS - 1:
             keep_own.start()
             keep_window.start()
+            for phase in range(1 + ITERS):
+                wait_sent(phase)
+            keep_window.wait()
+            keep_own.wait()
+            for di, dj in DIRS:
+
+                @pl.when(jnp.logical_not(exists(di, dj)))
+                def _(di=di, dj=dj):
+                    blank(di, dj).wait()
         if step == 0:
             wait_arrivals(1)
             for at in (0, 1):
@@ -426,21 +440,13 @@
         wait_arrivals(2 + step)
 
         if step < ITERS - 1:
-            total = band_gradient(grads.at[step], blocks, rows_ref, cols_ref)
+            spread = band_gradient(grads.at[step], blocks, rows_ref)
+            total = jnp.dot(spread, cols_ref[...], preferred_element_type=f32)
             for gi, (start, size) in enumerate(bands(core)):
                 at = slice(start, start + size)
                 scale = flag_row(grads.at[step], gi, core)
                 window[at, :] = jnp.clip(window[at, :] - STEP_SIZE * scale * total[at], -1.0, 1.0)
-    keep_window.wait()
-    keep_own.wait()
-    for di, dj in DIRS:
-
-        @pl.when(jnp.logical_not(exists(di, dj)))
-        def _(di=di, dj=dj):
-            blank(di, dj).wait()
-
-    for phase in range(2 + ITERS):
-        wait_sent(phase)
+    wait_sent(1 + ITERS)
 
 
 def body(axes, mask_field, resist_goal, kernels, colour, active):

time: 28.7 us -> 28.5 us (level)
  Pallas kernels: 26.6 us -> 26.3 us
where the time goes in v5:
time: 28.5 us; the launch traced here: 28.3 us
  Pallas kernels  26.3 us (92%)
  between operations  1.93 us (7%)
    pallas_call x1, Pallas kernels, body(): pl.pallas_call(functools.partial(kernel, axes, len(sources)), out_shape=(...  23 us
    pallas_call x1, Pallas kernels, body(): pl.pallas_call(finish, out_shape=(jax.ShapeDtypeStruct((core, core), f32)...  3.32 us

profile of v5, /device:TPU:1, one launch (start us, length us, event | category | flops | bytes accessed | tf_op | source)
XLA Modules:
  0.0 28.3 jit_solution(15963992093181564195)
XLA Ops:
  1.9 23.0 %shard_map.158 = (f32[512,512]{1,0:T(8,128)}, bf16[9,64,128]{2,1,0:T(8,128)(2,1)}) custom-call(s32[1,1]{1,0:T(1,128)S(6)} %copy.17.colour_ref, s32[1,1]{1,0:T(1,128)S(6)} %copy.18.active_ref, f32[384,384]{1,0:T(8,128)} %refs_0_.1, f32[384,384]{1,0:T(8,128)} %refs_1_.1, f32[8,128,64]{2,1,0:T(8,128)} %bitcast.1, bf16[128,512]{1,0:T(8,128)(2,1)} %constant.20.clone.refs_3_, ...), custom_call_target="tpu_custom_call" | custom-call | tf_op jit(solution)/shard_map/pallas_call | solution.py:462
  24.9 3.3 %shard_map.159 = (f32[384,384]{1,0:T(8,128)}, f32[512,512]{1,0:T(8,128)}) custom-call(bf16[9,64,128]{2,1,0:T(8,128)(2,1)} %get-tuple-element.4.last_ref, bf16[512,384]{1,0:T(8,128)(2,1)} %constant.28.clone.refs_11_.rows_src, bf16[384,512]{1,0:T(8,128)(2,1)} %constant.29.clone.refs_12_.cols_src, f32[512,512]{1,0:T(8,128)} %get-tuple-element.5.window_ref), custom_call_target="tpu_custom_call" | custom-call | tf_op jit(solution)/shard_map/pallas_call | solution.py:505
